TPU v7x, 32 devices: a whole 2x2x4 slice. The times are simulated.
32 devices in a mesh: groups: 2 (over y), lon: 4 (over z), lat: 2 (over core), member: 2 (over x).
Axes of the slice: x: 2, y: 2, z: 4, core: 2. Of those that a mesh axis runs over, the one named last changes fastest.
Arguments:
- latent: bfloat16 [4, 32, 256, 256], P(('groups', 'member'), 'lat', 'lon'), parts along dimension 0, may hold values from -6 to 6
- target: float32 [64, 256, 72], P(('groups', 'lat'), 'lon'), parts along dimension 0, may hold values from -6 to 6
- quadrature: bfloat16 [4, 32, 5, 17], replicated, may hold values from -0.625 to 0.625
- widths: int32 [32], replicated, may hold values from 1 to 8, as said below
- conv_weight: bfloat16 [1024, 256], replicated, may hold values from -0.1875 to 0.1875
- output_weight: bfloat16 [256, 72], replicated, may hold values from -0.375 to 0.375
Outputs:
- grad_latent: bfloat16 [4, 32, 256, 256], P(('groups', 'member'), 'lat', 'lon'), parts along dimension 0
- grad_conv: float32 [2048, 256], P('groups'), parts along dimension 0
- grad_out: float32 [512, 72], P('groups'), parts along dimension 0
There are 2 independent parts, one for each index of `groups`. A program takes and returns all parts, laid end to end along the dimension named above; an argument that names none is the same for every part. Nothing has to cross between parts.
Inputs may be any that keep to these rules, and one draw needn't show every extreme that they name: widths[0] equals 8 and the last row's width is 1.
All inputs are finite; a program needn't handle non-finite values.
Results may differ from a plain program's by a relative error of at most 0.012.
Values may be sent and summed in bfloat16 or wider, within the bound.
A program may use at most 64 MiB of HBM per device.

v0:
```python
import math

import jax
import jax.numpy as jnp
from jax import lax
from jax.sharding import PartitionSpec as P

smoothing = 0.1


def extended(block, sides, width, periodic):
    for axis, dim in sides:
        count = lax.axis_size(axis)
        forward = [(i, i + 1) for i in range(count - 1)]
        if periodic:
            forward.append((count - 1, 0))
        backward = [(target, source) for source, target in forward]
        low = lax.ppermute(
            lax.slice_in_dim(block, block.shape[dim] - width, None, axis=dim), axis, forward
        )
        high = lax.ppermute(lax.slice_in_dim(block, 0, width, axis=dim), axis, backward)
        block = jnp.concatenate([low, block, high], axis=dim)
    return block


def softened_slope(difference):
    return difference / jnp.sqrt(difference * difference + smoothing * smoothing)


def masked_filter(quadrature, widths):
    tap_count = quadrature.shape[3]
    half_taps = tap_count // 2
    offsets = jnp.abs(jnp.arange(tap_count) - half_taps)
    keep_mask = (offsets[None, :] <= widths[:, None]).astype(quadrature.dtype)
    return quadrature * keep_mask[None, :, None, :]


def local(latent, target, quadrature, widths, conv_weight, output_weight):
    latitude_rows = latent.shape[1]
    longitude_columns = latent.shape[2]
    channels = latent.shape[3]
    kernels = quadrature.shape[0]
    taps_lat = quadrature.shape[2]
    taps_lon = quadrature.shape[3]
    radius = taps_lat // 2
    half_lon = taps_lon // 2
    field_count = output_weight.shape[1]
    members = lax.axis_size("member")
    total_lat = latitude_rows * lax.axis_size("lat")
    total_lon = longitude_columns * lax.axis_size("lon")
    cell_count = latitude_rows * longitude_columns
    ext_cols = longitude_columns + 2 * half_lon
    rows_block = 8
    block_count = latitude_rows // rows_block
    row_start = lax.axis_index("lat") * latitude_rows
    psi_all = masked_filter(quadrature, widths)
    psi_padded = jnp.pad(psi_all, ((0, 0), (radius, radius), (0, 0), (0, 0)))
    psi_local = lax.dynamic_slice_in_dim(psi_padded, row_start + radius, latitude_rows, 1)
    psi_ext = lax.dynamic_slice_in_dim(psi_padded, row_start, latitude_rows + 2 * radius, 1)
    field_in = latent[0]
    lon_ext = extended(field_in, (("lon", 1),), half_lon, True)
    full_ext = extended(lon_ext, (("lat", 0),), radius, False)
    forward_hot = (
        jnp.arange(ext_cols)[None, None, :] - jnp.arange(longitude_columns)[None, :, None]
        == jnp.arange(taps_lon)[:, None, None]
    ).astype(jnp.bfloat16)

    def basis_block(block_id):
        first_row = block_id * rows_block
        coeff_blk = lax.dynamic_slice_in_dim(psi_local, first_row, rows_block, 1)
        toeplitz = jnp.einsum(
            "kiab,bje->ikjae", coeff_blk, forward_hot, preferred_element_type=jnp.float32
        ).astype(jnp.bfloat16)
        stacked = jnp.stack(
            [
                lax.dynamic_slice_in_dim(full_ext, first_row + offset, rows_block, 0)
                for offset in range(taps_lat)
            ],
            axis=1,
        )
        return jnp.einsum(
            "ikjae,iaec->ijkc", toeplitz, stacked, preferred_element_type=jnp.float32
        ).astype(jnp.bfloat16)

    basis_all = lax.map(basis_block, jnp.arange(block_count)).reshape(
        cell_count, kernels * channels
    )
    hidden = jnp.dot(basis_all, conv_weight, preferred_element_type=jnp.float32)
    blended_rows = (
        field_in.reshape(cell_count, channels).astype(jnp.float32) + jax.nn.gelu(hidden)
    ).astype(jnp.bfloat16)
    predicted_state = jnp.dot(
        blended_rows, output_weight, preferred_element_type=jnp.float32
    ).astype(jnp.bfloat16)
    predicted_state = predicted_state.reshape(1, latitude_rows, longitude_columns, field_count)
    member_batch = lax.all_gather(predicted_state, "member", axis=0, tiled=True).astype(jnp.float32)
    member_prediction = predicted_state[0].astype(jnp.float32)
    pairwise_sum = jnp.sum(softened_slope(member_prediction[None] - member_batch), axis=0)
    prediction_gradient = (
        softened_slope(member_prediction - target) - pairwise_sum / (members - 1)
    ).astype(jnp.bfloat16)
    grad_flat = prediction_gradient.reshape(cell_count, field_count)
    up_grad = lax.dot_general(
        grad_flat, output_weight, (((1,), (1,)), ((), ())), preferred_element_type=jnp.float32
    )
    hid_grad = jax.vjp(jax.nn.gelu, hidden)[1](up_grad)[0].astype(jnp.bfloat16)
    conv_local = lax.dot_general(
        basis_all, hid_grad, (((0,), (0,)), ((), ())), preferred_element_type=jnp.float32
    )
    out_local = lax.dot_general(
        blended_rows, grad_flat, (((0,), (0,)), ((), ())), preferred_element_type=jnp.float32
    )
    conv_total, out_total = lax.psum((conv_local, out_local), ("lon", "lat", "member"))
    norm_scale = 1.0 / math.sqrt(members * total_lat * total_lon)
    grad_conv = conv_total * norm_scale
    grad_out = out_total * norm_scale
    basis_grad = lax.dot_general(
        hid_grad, conv_weight, (((1,), (1,)), ((), ())), preferred_element_type=jnp.float32
    ).astype(jnp.bfloat16)
    basis_grad = basis_grad.reshape(latitude_rows, longitude_columns, kernels * channels)
    lon_grad = extended(basis_grad, (("lon", 1),), half_lon, True)
    grad_ext = extended(lon_grad, (("lat", 0),), radius, False)
    grad_cells = grad_ext.reshape(latitude_rows + 2 * radius, ext_cols, kernels, channels)
    back_hot = (
        jnp.arange(longitude_columns)[None, None, :]
        + 2 * half_lon
        - jnp.arange(ext_cols)[None, :, None]
        == jnp.arange(taps_lon)[:, None, None]
    ).astype(jnp.bfloat16)

    def adjoint_block(block_id):
        first_row = block_id * rows_block
        accum_sum = jnp.zeros((rows_block, longitude_columns, channels), jnp.float32)
        for offset in range(taps_lat):
            start_row = first_row + 2 * radius - offset
            coeff_blk = lax.dynamic_slice_in_dim(psi_ext, start_row, rows_block, 1)[:, :, offset, :]
            toeplitz = jnp.einsum(
                "kib,bsq->iksq", coeff_blk, back_hot, preferred_element_type=jnp.float32
            ).astype(jnp.bfloat16)
            window = lax.dynamic_slice_in_dim(grad_cells, start_row, rows_block, 0)
            accum_sum = accum_sum + jnp.einsum(
                "iksq,iskc->iqc", toeplitz, window, preferred_element_type=jnp.float32
            )
        return accum_sum

    adjoint = lax.map(adjoint_block, jnp.arange(block_count)).reshape(
        latitude_rows, longitude_columns, channels
    )
    grad_latent = (up_grad.reshape(latitude_rows, longitude_columns, channels) + adjoint).astype(
        jnp.bfloat16
    )[None]
    return (grad_latent, grad_conv, grad_out)


def solution(mesh):
    in_specs = (
        P(("groups", "member"), "lat", "lon", None),
        P(("groups", "lat"), "lon", None),
        P(),
        P(),
        P(),
        P(),
    )
    out_specs = (P(("groups", "member"), "lat", "lon", None), P("groups", None), P("groups", None))
    return jax.shard_map(local, mesh=mesh, in_specs=in_specs, out_specs=out_specs, check_vma=False)
```

profile of v0, /device:TPU:0, one launch (start us, length us, event | category | flops | bytes accessed | tf_op | source)
XLA Modules:
  0.0 198.3 jit_solution(14841324513859976990)
XLA Ops:
  8.2 3.1 %collective-permute-start = (bf16[16,8,256]{2,1,0:T(8,128)(2,1)S(1)}, bf16[16,8,256]{2,1,0:T(8,128)(2,1)S(1)}, u32[]{:S(2)}, u32[]{:S(2)}) collective-permute-start(bf16[16,8,256]{2,1,0:T(8,128)(2,1)S(1)} %get-tuple-element.361), channel_id=1, source_target_pairs={{0,4},{4,8},{8,12},{12,0},{1,5},{5,9},{9,13},{13,1},{2,6},{6,10},{... | collective-permute-start | bytes 196616 | tf_op jit(solution)/shard_map/ppermute | solution.py:18
  11.3 2.1 %collective-permute-start.1 = (bf16[16,8,256]{2,1,0:T(8,128)(2,1)S(1)}, bf16[16,8,256]{2,1,0:T(8,128)(2,1)S(1)}, u32[]{:S(2)}, u32[]{:S(2)}) collective-permute-start(bf16[16,8,256]{2,1,0:T(8,128)(2,1)S(1)} %get-tuple-element.362), channel_id=1, source_target_pairs={{4,0},{8,4},{12,8},{0,12},{5,1},{9,5},{13,9},{1,13},{6,2},{10,6},{... | collective-permute-start | bytes 196616 | tf_op jit(solution)/shard_map/ppermute | solution.py:21
  13.4 1.1 copy.45
  17.6 1.5 collective-permute-start.2
  19.0 1.3 collective-permute-start.3
  20.4 1.8 collective-permute-done.3
  22.3 12.0 %while.29 = (s32[]{:T(128)}, bf16[2,8,64,4,256]{4,3,2,1,0:T(4,128)(2,1)}, s32[2]{0:T(128)S(1)}, bf16[20,80,256]{2,1,0:T(8,128)(2,1)S(1)}, bf16[4,16,5,17]{3,1,0,...) while((s32[]{:T(128)}, ...), condition=%wide.region_1.2_spmd.clone, body=%wide.region_0.1_spmd.clone.sunk | while | flops 448800768 | bytes 11400136 | solution.py:85
  23.8 1.6 convert_bitcast_fusion.2
  25.4 1.1 fusion.152
  26.5 1.8 copy_dynamic-update-slice_fusion.2
  29.8 1.6 convert_bitcast_fusion.2
  31.4 1.1 fusion.152
  32.5 1.8 copy_dynamic-update-slice_fusion.2
  34.2 2.1 %copy.75 = bf16[128,8,4,256]{3,1,2,0:T(8,128)(2,1)S(1)} copy(bf16[128,8,4,256]{3,2,1,0:T(4,128)(2,1)} %bitcast.72) | data formatting | bytes 4194304
  36.4 1.9 fusion.102
  38.9 9.0 %all_gather.3 = bf16[2,16,64,72]{3,2,1,0:T(8,128)(2,1)S(1)} all-gather(bf16[1,16,64,72]{3,2,1,0:T(8,128)(2,1)S(1)} %bitcast.236), channel_id=1, replica_groups=mesh['groups'=2,'lon'=4,'lat'=2,'member'=2] {'member'}, dimensions={0}, use_global_device_ids=true | all-gather | bytes 442368 | tf_op jit(solution)/shard_map/all_gather | solution.py:96
  49.2 1.7 fusion.101
  50.9 1.7 fusion.106
  54.9 3.1 %collective-permute-start.5 = (bf16[16,8,1024]{2,1,0:T(8,128)(2,1)S(1)}, bf16[16,8,1024]{2,1,0:T(8,128)(2,1)S(1)}, u32[]{:S(2)}, u32[]{:S(2)}) collective-permute-start(bf16[16,8,1024]{2,1,0:T(8,128)(2,1)S(1)} %get-tuple-element.358), channel_id=1, source_target_pairs={{4,0},{8,4},{12,8},{0,12},{5,1},{9,5},{13,9},{1,13},{6,2},{10,6},{... | collective-permute-start | bytes 786440 | tf_op jit(solution)/shard_map/ppermute | solution.py:21
  58.0 8.6 %collective-permute-done.4 = bf16[16,8,1024]{2,1,0:T(8,128)(2,1)S(1)} collective-permute-done((bf16[16,8,1024]{2,1,0:T(8,128)(2,1)}, bf16[16,8,1024]{2,1,0:T(8,128)(2,1)S(1)}, u32[]{:S(2)}, u32[]{:S(2)}) %collective-permute-start.4) | collective-permute-done | bytes 262176 | tf_op jit(solution)/shard_map/ppermute | solution.py:18
  66.7 4.1 %collective-permute-done.5 = bf16[16,8,1024]{2,1,0:T(8,128)(2,1)S(1)} collective-permute-done((bf16[16,8,1024]{2,1,0:T(8,128)(2,1)S(1)}, bf16[16,8,1024]{2,1,0:T(8,128)(2,1)S(1)}, u32[]{:S(2)}, u32[]{:S(2)}) %collective-permute-start.5) | collective-permute-done | bytes 262176 | tf_op jit(solution)/shard_map/ppermute | solution.py:21
  71.6 1.3 collective-permute-start.6
  72.9 1.5 collective-permute-start.7
  74.4 75.7 %all-reduce.4.cloned.1.call-done = (f32[1024,256]{1,0:T(8,128)}, f32[256,72]{0,1:T(8,128)}) async-done(((f32[1024,256]{1,0:T(8,128)}, f32[256,72]{0,1:T(8,128)}), (f32[1024,256]{1,0:T(8,128)}, f32[256,72]{0,1:T(8,128)})) %all-reduce.4.cloned.1.call-update) | async-done | bytes 1122320 | tf_op jit(solution)/shard_map/psum | solution.py:113
  150.1 1.5 broadcast_multiply_fusion.2
  151.6 2.3 %broadcast_multiply_fusion = f32[1024,256]{1,0:T(8,128)} fusion(f32[1024,256]{1,0:T(8,128)} %get-tuple-element.353), kind=kLoop, calls=%fused_computation.98 | loop fusion | flops 262144 | bytes 2097152 | tf_op jit(solution)/shard_map/mul | solution.py:115
  153.9 1.3 pad_maximum_fusion
  155.2 2.0 copy.96
  157.2 32.1 %while.30 = (s32[]{:T(128)}, f32[2,8,64,256]{3,2,1,0:T(8,128)}, s32[2]{0:T(128)S(1)}, bf16[4,20,5,17]{3,1,0,2:T(8,128)(2,1)}, bf16[20,80,4,256]{3,1,2,0:T(8,128)...) while((s32[]{:T(128)}, f32[2,8,64,256]{3,2,1,0:T(8,128)}, ...), condition=%wide.region_4.5_spmd.clone.clone, body=%wide.region_3.4_spmd.clone.clone.sunk | while | flops 449497088 | bytes 14693399 | solution.py:146
  159.5 1.8 fusion.169
  161.2 1.0 fusion.170
  162.3 1.8 fusion.171
  164.1 1.0 fusion.172
  165.1 1.8 fusion.173
  166.9 1.0 fusion.174
  167.9 1.8 fusion.175
  169.7 1.0 fusion.176
  170.7 2.6 %fusion.177 = f32[2,8,64,256]{3,2,1,0:T(8,128)} fusion(f32[2,8,64,256]{3,2,1,0:T(8,128)} %get-tuple-element.517, s32[]{:T(128)} %get-tuple-element.516, f32[8,64,256]{2,1,0:T(8,128)S(1)} %fusion.175, bf16[20,80,4,256]{3,1,2,0:T(8,128)(2,1)} %get-tuple-element.541, s32[]{:T(128)S(6)} %select_n.131, bf16[8,4,80,64]{2,0,3,1:T(8,128)(2,1)S(1)} %fusion.176), kind=kOutput, calls=%fused_computation.47.clone.1 | convolution fusion | flops 84017152 | bytes 2687492 | tf_op jit(solution)/shard_map/while/body/eval_jaxpr/iksq,iskc->iqc/dot_general | solution.py:141
  174.5 1.0 fusion.168
  175.5 1.8 fusion.169
  177.3 1.0 fusion.170
  178.3 1.8 fusion.171
  180.1 1.0 fusion.172
  181.1 1.8 fusion.173
  184.0 1.8 fusion.175
  185.7 1.0 fusion.176
  186.8 2.6 %fusion.177 = f32[2,8,64,256]{3,2,1,0:T(8,128)} fusion(f32[2,8,64,256]{3,2,1,0:T(8,128)} %get-tuple-element.517, s32[]{:T(128)} %get-tuple-element.516, f32[8,64,256]{2,1,0:T(8,128)S(1)} %fusion.175, bf16[20,80,4,256]{3,1,2,0:T(8,128)(2,1)} %get-tuple-element.541, s32[]{:T(128)S(6)} %select_n.131, bf16[8,4,80,64]{2,0,3,1:T(8,128)(2,1)S(1)} %fusion.176), kind=kOutput, calls=%fused_computation.47.clone.1 | convolution fusion | flops 84017152 | bytes 2687492 | tf_op jit(solution)/shard_map/while/body/eval_jaxpr/iksq,iskc->iqc/dot_general | solution.py:141
  189.3 2.1 %fusion.103 = bf16[1,16,64,256]{3,2,1,0:T(8,128)(2,1)} fusion(f32[1,16,64,256]{3,2,1,0:T(8,128)S(1)} %bitcast.237, f32[1,16,64,256]{3,2,1,0:T(8,128)} %bitcast.238), kind=kLoop, calls=%fused_computation.95 | loop fusion | flops 524288 | bytes 2621440 | tf_op jit(solution)/shard_map/convert_element_type | solution.py:149
  (64 shorter events, 13.9 us)
Async XLA Ops:
  7.2 29.2 %copy-start = (bf16[1024,256]{1,0:T(8,128)(2,1)S(1)}, bf16[1024,256]{1,0:T(8,128)(2,1)}, u32[]{:S(2)}) copy-start(bf16[1024,256]{1,0:T(8,128)(2,1)} %param.14) | copy-start | bytes 1572868
  7.2 15.0 %copy-start.1 = (bf16[1,16,64,256]{3,2,1,0:T(8,128)(2,1)S(1)}, bf16[1,16,64,256]{3,2,1,0:T(8,128)(2,1)}, u32[]{:S(2)}) copy-start(bf16[1,16,64,256]{3,2,1,0:T(8,128)(2,1)} %param.10) | copy-start | bytes 1572868
  7.2 142.9 %all-reduce.4.cloned.1.call-start = ((), (), s32[]{:S(2)}) async-start(), calls=%async_computation | async-start | bytes 2244608 | tf_op jit(solution)/shard_map/psum | solution.py:113
  8.2 8.5 %collective-permute-start = (bf16[16,8,256]{2,1,0:T(8,128)(2,1)S(1)}, bf16[16,8,256]{2,1,0:T(8,128)(2,1)S(1)}, u32[]{:S(2)}, u32[]{:S(2)}) collective-permute-start(bf16[16,8,256]{2,1,0:T(8,128)(2,1)S(1)} %get-tuple-element.361), channel_id=1, source_target_pairs={{0,4},{4,8},{8,12},{12,0},{1,5},{5,9},{9,13},{13,1},{2,6},{6,10},{... | collective-permute-start | bytes 196616 | tf_op jit(solution)/shard_map/ppermute | solution.py:18
  11.3 5.4 %collective-permute-start.1 = (bf16[16,8,256]{2,1,0:T(8,128)(2,1)S(1)}, bf16[16,8,256]{2,1,0:T(8,128)(2,1)S(1)}, u32[]{:S(2)}, u32[]{:S(2)}) collective-permute-start(bf16[16,8,256]{2,1,0:T(8,128)(2,1)S(1)} %get-tuple-element.362), channel_id=1, source_target_pairs={{4,0},{8,4},{12,8},{0,12},{5,1},{9,5},{13,9},{1,13},{6,2},{10,6},{... | collective-permute-start | bytes 196616 | tf_op jit(solution)/shard_map/ppermute | solution.py:21
  17.6 2.8 %collective-permute-start.2 = (bf16[2,80,256]{2,1,0:T(8,128)(2,1)S(1)}, bf16[2,80,256]{2,1,0:T(8,128)(2,1)S(1)}, u32[]{:S(2)}, u32[]{:S(2)}) collective-permute-start(bf16[2,80,256]{2,1,0:T(8,128)(2,1)S(1)} %get-tuple-element.359), channel_id=1, source_target_pairs={{0,2},{1,3},{4,6},{5,7},{8,10},{9,11},{12,14},{13,15},{16,18},{17,... | collective-permute-start | bytes 245768 | tf_op jit(solution)/shard_map/ppermute | solution.py:18
  19.0 3.2 %collective-permute-start.3 = (bf16[2,80,256]{2,1,0:T(8,128)(2,1)S(1)}, bf16[2,80,256]{2,1,0:T(8,128)(2,1)S(1)}, u32[]{:S(2)}, u32[]{:S(2)}) collective-permute-start(bf16[2,80,256]{2,1,0:T(8,128)(2,1)S(1)} %get-tuple-element.360), channel_id=1, source_target_pairs={{2,0},{3,1},{6,4},{7,5},{10,8},{11,9},{14,12},{15,13},{18,16},{19,... | collective-permute-start | bytes 245768 | tf_op jit(solution)/shard_map/ppermute | solution.py:21
  36.3 1.9 copy-start.2
  36.4 1.9 copy-start.6
  38.3 9.9 %copy-start.5 = (f32[16,64,72]{2,1,0:T(8,128)S(1)}, f32[16,64,72]{2,1,0:T(8,128)}, u32[]{:S(2)}) copy-start(f32[16,64,72]{2,1,0:T(8,128)} %param.11) | copy-start | bytes 884740
  47.9 1.3 copy-start.7
  49.2 1.7 copy-start.3
  54.1 12.5 %collective-permute-start.4 = (bf16[16,8,1024]{2,1,0:T(8,128)(2,1)}, bf16[16,8,1024]{2,1,0:T(8,128)(2,1)S(1)}, u32[]{:S(2)}, u32[]{:S(2)}) collective-permute-start(bf16[16,8,1024]{2,1,0:T(8,128)(2,1)} %get-tuple-element.357), channel_id=1, source_target_pairs={{0,4},{4,8},{8,12},{12,0},{1,5},{5,9},{9,13},{13,1},{2,6},{6,10},{... | collective-permute-start | bytes 786440 | tf_op jit(solution)/shard_map/ppermute | solution.py:18
  54.9 15.8 %collective-permute-start.5 = (bf16[16,8,1024]{2,1,0:T(8,128)(2,1)S(1)}, bf16[16,8,1024]{2,1,0:T(8,128)(2,1)S(1)}, u32[]{:S(2)}, u32[]{:S(2)}) collective-permute-start(bf16[16,8,1024]{2,1,0:T(8,128)(2,1)S(1)} %get-tuple-element.358), channel_id=1, source_target_pairs={{4,0},{8,4},{12,8},{0,12},{5,1},{9,5},{13,9},{1,13},{6,2},{10,6},{... | collective-permute-start | bytes 786440 | tf_op jit(solution)/shard_map/ppermute | solution.py:21
  71.6 82.3 %collective-permute-start.6 = (bf16[2,80,1024]{2,1,0:T(8,128)(2,1)}, bf16[2,80,1024]{2,1,0:T(8,128)(2,1)S(1)}, u32[]{:S(2)}, u32[]{:S(2)}) collective-permute-start(bf16[2,80,1024]{2,1,0:T(8,128)(2,1)} %get-tuple-element.355), channel_id=1, source_target_pairs={{0,2},{1,3},{4,6},{5,7},{8,10},{9,11},{12,14},{13,15},{16,18},{17,... | collective-permute-start | bytes 983048 | tf_op jit(solution)/shard_map/ppermute | solution.py:18
  72.9 81.0 %collective-permute-start.7 = (bf16[2,80,1024]{2,1,0:T(8,128)(2,1)}, bf16[2,80,1024]{2,1,0:T(8,128)(2,1)}, u32[]{:S(2)}, u32[]{:S(2)}) collective-permute-start(bf16[2,80,1024]{2,1,0:T(8,128)(2,1)} %get-tuple-element.356), channel_id=1, source_target_pairs={{2,0},{3,1},{6,4},{7,5},{10,8},{11,9},{14,12},{15,13},{18,16},{19,... | collective-permute-start | bytes 983048 | tf_op jit(solution)/shard_map/ppermute | solution.py:21
  157.2 32.1 %copy-start.4 = (f32[1024,256]{1,0:T(8,128)S(1)}, f32[1024,256]{1,0:T(8,128)}, u32[]{:S(2)}) copy-start(f32[1024,256]{1,0:T(8,128)} %get-tuple-element.366) | copy-start | bytes 3145732
Sparse Core Ops, SparseCore 0:
  53.5 96.5 all-reduce.3
where the time goes:
time: 200 us; the launch traced here: 198 us
  waiting for transfers between devices  90.3 us (45%)
  matrix products  42 us (21%)
  local copies, waits for them, and re-layouts  14.9 us (7%)
  starting transfers between devices  14.6 us (7%)
  between operations  14.2 us (7%)
  other arithmetic  10.3 us (5%)
  blocking collectives  9.04 us (5%)
  loops' own time  3.04 us (2%)
    psum x1, waiting for transfers between devices, local(): lax.psum((conv_local, out_local), ('lon', 'lat', 'member'))  75.7 us
    dot_general x10, matrix products, adjoint_block(): jnp.einsum('iksq,iskc->iqc', toeplitz, window, preferred_element_type=jnp...  19.2 us
    dot_general x10, matrix products, adjoint_block(): jnp.einsum('kib,bsq->iksq', coeff_blk, back_hot, preferred_element_type=j...  10.2 us
    all_gather x1, blocking collectives, local(): lax.all_gather(predicted_state, 'member', axis=0, tiled=True)  9.04 us
    ppermute x4, waiting for transfers between devices, extended(): lax.ppermute(lax.slice_in_dim(block, block.shape[dim] - width, None, axis...  8.61 us
    ppermute x4, starting transfers between devices, extended(): lax.ppermute(lax.slice_in_dim(block, 0, width, axis=dim), axis, backward)  7.92 us
    ppermute x4, starting transfers between devices, extended(): lax.ppermute(lax.slice_in_dim(block, block.shape[dim] - width, None, axis...  6.6 us
    ppermute x4, waiting for transfers between devices, extended(): lax.ppermute(lax.slice_in_dim(block, 0, width, axis=dim), axis, backward)  5.93 us
  transfers between devices with their start and end apart: 9, of which 4 were waited for; matrix products, arithmetic and copies ran while one was open for 4% of the time, Pallas kernels for 0%

commit v1 on v0

v1 whole, which is shorter than its diff:
```python
import functools
import math

import jax
import jax.numpy as jnp
from jax import lax
from jax.experimental import pallas as pl
from jax.experimental.pallas import tpu as pltpu
from jax.sharding import PartitionSpec as P

smoothing = 0.1
MESH = pl.DeviceIdType.MESH
f32 = jnp.float32
bf16 = jnp.bfloat16
CHUNKS = 4


def slope(d):
    return d * lax.rsqrt(d * d + smoothing * smoothing)


def dims_of(rows, cols, taps_lat, half):
    pitch = cols + 2 * half
    slots = rows + taps_lat - 1
    window = -(-(16 + taps_lat * pitch) // 128) * 128
    return pitch, slots, window, (rows - 1) * pitch + window


def kernel(sizes, lat_ref, tgt_ref, base_ref, cw_ref, ow_ref, gl_ref, gc_ref, go_ref,
           T, X, G, basis, BG, DG, mixed, F, FR, wo, pg, hg, GF, GB, GA,
           SL, SR, RL, RR, RC, SL2, SR2, SC2, QL, QR, QC, QLd, QRd, R1, R2, R3,
           hs, hr, fs, fr, as_, ar, s1s, s1r, s2s, s2r, s3s, s3r, a3s, a3r, a2s, a2r, a1s, a1r):
    rows, cols, C, K, taps_lat, half, L, M, fields, scale = sizes
    radius = taps_lat // 2
    pitch, slots, window, span = dims_of(rows, cols, taps_lat, half)
    n = rows * cols
    per = rows // CHUNKS
    cn = per * cols
    lat = lax.axis_index("lat")
    lon = lax.axis_index("lon")
    mem = lax.axis_index("member")
    other = 1 - lat
    right = lax.rem(lon + 1, L)
    left = lax.rem(lon + L - 1, L)
    hh = radius * half

    def rcopy(src, dst, ss, rs, dev):
        return pltpu.make_async_remote_copy(
            src_ref=src, dst_ref=dst, send_sem=ss, recv_sem=rs, device_id=dev, device_id_type=MESH)

    barrier = pltpu.get_barrier_semaphore()
    peers = [{"lat": other}, {"lat": other, "lon": left}, {"lat": other, "lon": right}]
    peers += [{"lon": lax.rem(lon + d, L)} for d in range(1, L)]
    peers += [{"member": lax.rem(mem + d, M)} for d in range(1, M)]
    for dev in peers:
        pl.semaphore_signal(barrier, inc=1, device_id=dev, device_id_type=MESH)

    lat3 = lat_ref[...].astype(f32).reshape(rows, cols, C)
    SL[...] = lat3[:, :half].reshape(rows * half, C).astype(bf16)
    SR[...] = lat3[:, cols - half:].reshape(rows * half, C).astype(bf16)
    zero_halo = jnp.zeros((hh, C), bf16)
    edge = pl.multiple_of(lat * (hh + rows * half), 16)
    RL[pl.ds(edge, hh), :] = zero_halo
    RR[pl.ds(edge, hh), :] = zero_halo
    pl.semaphore_wait(barrier, len(peers))

    near = pl.multiple_of(other * (rows - radius) * half, 16)
    far = pl.multiple_of(lat * 0 + (1 - other) * (hh + rows * half), 16)
    nearrow = pl.multiple_of(other * (rows - radius) * cols, 16)
    inner = pl.ds(hh, rows * half)
    halo = [
        rcopy(SL, RR.at[inner], hs.at[0], hr.at[0], {"lon": left}),
        rcopy(SR, RL.at[inner], hs.at[1], hr.at[1], {"lon": right}),
        rcopy(SL.at[pl.ds(near, hh)], RR.at[pl.ds(far, hh)], hs.at[2], hr.at[2], {"lat": other, "lon": left}),
        rcopy(SR.at[pl.ds(near, hh)], RL.at[pl.ds(far, hh)], hs.at[3], hr.at[3], {"lat": other, "lon": right}),
        rcopy(lat_ref.at[pl.ds(nearrow, radius * cols)], RC, hs.at[4], hr.at[4], {"lat": other}),
    ]
    for c in halo:
        c.start()

    def build(i, carry):
        rowsb = base_ref[pl.ds(pl.multiple_of(i * 8, 8), 8), :]
        for k in range(K):
            line = jnp.broadcast_to(rowsb[k:k + 1, :], (cols, window))
            T[i, k * cols:(k + 1) * cols, :] = pltpu.roll(line, 0, 1, stride=1, stride_axis=0).astype(bf16)
        return carry
    lax.fori_loop(0, rows, build, 0)

    G[...] = jnp.zeros(G.shape, f32)
    wo[...] = jnp.zeros(wo.shape, bf16)
    wo[:, :fields] = ow_ref[...]
    pg[...] = jnp.zeros(pg.shape, bf16)
    X[pl.ds(16 + slots * pitch, span - 16 - slots * pitch), :] = jnp.zeros((span - 16 - slots * pitch, C), bf16)
    for r in range(rows):
        X[16 + pitch * (r + radius):16 + pitch * (r + radius) + cols, :] = lat_ref[r * cols:(r + 1) * cols, :]
    zrow = jnp.zeros((cols, C), bf16)
    for r in range(radius):
        X[pl.ds(pl.multiple_of(16 + pitch * (r + lat * (rows + radius)), 16), cols), :] = zrow
    for c in halo:
        c.wait()
    for r in range(radius):
        X[pl.ds(pl.multiple_of(16 + pitch * (r + other * (rows + radius)), 16), cols), :] = RC[r * cols:(r + 1) * cols, :]
    rl = RL[...].astype(f32)
    rr = RR[...].astype(f32)
    z8 = jnp.zeros((half, C), f32)
    X[0:16, :] = jnp.concatenate([z8, rl[0:half]], axis=0).astype(bf16)
    for r in range(slots):
        nxt = rl[(r + 1) * half:(r + 2) * half] if r + 1 < slots else z8
        X[16 + pitch * r + cols:16 + pitch * (r + 1), :] = jnp.concatenate(
            [rr[r * half:(r + 1) * half], nxt], axis=0).astype(bf16)

    c0 = math.sqrt(2 / math.pi)
    fcopies = []
    for ch in range(CHUNKS):
        def conv(ii, carry, ch=ch):
            i = ch * per + ii
            out = jnp.dot(T[i], X[pl.ds(pl.multiple_of(i * pitch, 16), window), :], preferred_element_type=f32).astype(bf16)
            for k in range(K):
                basis[pl.ds(pl.multiple_of(i * cols, 16), cols), k * C:(k + 1) * C] = out[k * cols:(k + 1) * cols]
            return carry
        lax.fori_loop(0, per, conv, 0, unroll=True)
        sl = slice(ch * cn, (ch + 1) * cn)
        h = jnp.dot(basis[sl, :], cw_ref[...], preferred_element_type=f32)
        t = jnp.tanh(c0 * (h + 0.044715 * h * h * h))
        DG[sl, :] = 0.5 * (1 + t) + 0.5 * h * (1 - t * t) * (c0 * (1 + 3 * 0.044715 * h * h))
        mx = (lat_ref[sl, :].astype(f32) + 0.5 * h * (1 + t)).astype(bf16)
        mixed[sl, :] = mx
        F[sl, :] = jnp.dot(mx, wo[...], preferred_element_type=f32).astype(bf16)
        cs = []
        for d in range(1, M):
            c = rcopy(F.at[pl.ds(ch * cn, cn)], FR.at[d - 1, pl.ds(ch * cn, cn)], fs.at[d - 1, ch], fr.at[d - 1, ch],
                      {"member": lax.rem(mem + d, M)})
            c.start()
            cs.append(c)
        fcopies.append(cs)

    for ch in range(CHUNKS):
        sl = slice(ch * cn, (ch + 1) * cn)
        mine = F[sl, :fields].astype(f32)
        first = slope(mine - tgt_ref[sl, :])
        for c in fcopies[ch]:
            c.wait()
        pair = jnp.zeros_like(mine)
        for d in range(1, M):
            pair = pair + slope(mine - FR[d - 1, sl, :fields].astype(f32))
        pg[sl, :fields] = (first - pair * (1.0 / (M - 1))).astype(bf16)
        up = lax.dot_general(pg[sl, :], wo[...], (((1,), (1,)), ((), ())), preferred_element_type=f32)
        for ii in range(per):
            r = ch * per + ii + radius
            G[16 + pitch * r:16 + pitch * r + cols, :] = up[ii * cols:(ii + 1) * cols]
        hg[sl, :] = (up * DG[sl, :]).astype(bf16)

    KC = K * C
    hc = C // 2
    total = 2 * KC + C
    tn = (((0,), (0,)), ((), ()))
    hgv = hg[...]
    for k in range(K):
        g = lax.dot_general(basis[:, k * C:(k + 1) * C], hgv, tn, preferred_element_type=f32)
        for half_id in range(2):
            part = g[:, half_id * hc:(half_id + 1) * hc]
            at = half_id * KC + k * C
            GF[at:at + C, :] = part
            GB[at:at + C, :] = part.astype(bf16)
    g = lax.dot_general(mixed[...], pg[...], tn, preferred_element_type=f32)
    GF[2 * KC:total, :] = g
    GB[2 * KC:total, :] = g.astype(bf16)

    n1 = total // 2
    n2 = n1 // M
    scatter = n2 % (16 * L) == 0
    n3 = n2 // L if scatter else n2
    o1 = pl.multiple_of(lat * n1, 16)
    o1o = pl.multiple_of(other * n1, 16)
    st1 = rcopy(GB.at[pl.ds(o1o, n1)], R1, s1s, s1r, {"lat": other})
    st1.start()

    def adjoint(first_row, last_row):
        lo, size = first_row * cols, (last_row - first_row) * cols
        BG[lo:lo + size, :] = lax.dot_general(
            hg[lo:lo + size, :], cw_ref[...], (((1,), (1,)), ((), ())), preferred_element_type=f32).astype(bf16)

        def body(i, carry):
            at = pl.ds(pl.multiple_of(i * cols, 16), cols)
            stacked = jnp.concatenate([BG[at, k * C:(k + 1) * C] for k in range(K)], axis=0)
            out = lax.dot_general(T[i], stacked, tn, preferred_element_type=f32)
            w = pl.ds(pl.multiple_of(i * pitch, 16), window)
            G[w, :] = G[w, :] + out
            return carry
        lax.fori_loop(first_row, last_row, body, 0)

    adjoint(0, rows // 2)

    st1.wait()
    v = GF[pl.ds(o1, n1), :] + R1[...].astype(f32)
    GF[pl.ds(o1, n1), :] = v
    GB[pl.ds(o1, n1), :] = v.astype(bf16)
    st2 = []
    for d in range(1, M):
        q = lax.rem(mem + d, M)
        c = rcopy(GB.at[pl.ds(pl.multiple_of(o1 + q * n2, 16), n2)], R2.at[d - 1], s2s.at[d - 1], s2r.at[d - 1], {"member": q})
        c.start()
        st2.append(c)

    adjoint(rows // 2, rows)
    for r in range(slots):
        pass
    SR2[...] = jnp.concatenate([G[16 + pitch * r + cols:16 + pitch * r + cols + half, :] for r in range(slots)], axis=0).astype(bf16)
    SL2[...] = jnp.concatenate([G[16 + pitch * r - half:16 + pitch * r, :] for r in range(slots)], axis=0).astype(bf16)
    for r in range(radius):
        SC2[r * cols:(r + 1) * cols, :] = G[pl.ds(pl.multiple_of(16 + pitch * (r + other * (rows + radius)), 16), cols), :].astype(bf16)
    beyond = pl.multiple_of(other * (hh + rows * half), 16)
    back = [
        rcopy(SR2.at[inner], QL, as_.at[0], ar.at[0], {"lon": right}),
        rcopy(SL2.at[inner], QR, as_.at[1], ar.at[1], {"lon": left}),
        rcopy(SR2.at[pl.ds(beyond, hh)], QLd, as_.at[2], ar.at[2], {"lat": other, "lon": right}),
        rcopy(SL2.at[pl.ds(beyond, hh)], QRd, as_.at[3], ar.at[3], {"lat": other, "lon": left}),
        rcopy(SC2, QC, as_.at[4], ar.at[4], {"lat": other}),
    ]
    for c in back:
        c.start()

    for c in st2:
        c.wait()
    o2 = pl.multiple_of(o1 + mem * n2, 16)
    v = GF[pl.ds(o2, n2), :]
    for d in range(1, M):
        v = v + R2[d - 1].astype(f32)
    GF[pl.ds(o2, n2), :] = v
    GB[pl.ds(o2, n2), :] = v.astype(bf16)
    st3 = []
    for d in range(1, L):
        q = lax.rem(lon + d, L)
        src = GB.at[pl.ds(pl.multiple_of(o2 + q * n3, 16), n3)] if scatter else GB.at[pl.ds(o2, n2)]
        dst = R3.at[d - 1] if scatter else R3.at[lon]
        c = rcopy(src, dst, s3s.at[d - 1], s3r.at[d - 1], {"lon": q})
        c.start()
        st3.append(c)

    for c in back:
        c.wait()
    ql = QL[...].astype(f32)
    qr = QR[...].astype(f32)
    qld = QLd[...].astype(f32)
    qrd = QRd[...].astype(f32)
    for r in range(rows):
        at = 16 + pitch * (r + radius)
        G[at:at + half, :] = G[at:at + half, :] + ql[r * half:(r + 1) * half]
        G[at + cols - half:at + cols, :] = G[at + cols - half:at + cols, :] + qr[r * half:(r + 1) * half]
    for r in range(radius):
        at = 16 + pitch * (radius + r + other * (rows - radius))
        w = pl.ds(pl.multiple_of(at, 16), cols)
        G[w, :] = G[w, :] + QC[r * cols:(r + 1) * cols, :].astype(f32)
        w = pl.ds(pl.multiple_of(at, 8), half)
        G[w, :] = G[w, :] + qld[r * half:(r + 1) * half]
        w = pl.ds(pl.multiple_of(at + cols - half, 8), half)
        G[w, :] = G[w, :] + qrd[r * half:(r + 1) * half]
    for r in range(rows):
        at = 16 + pitch * (r + radius)
        gl_ref[r * cols:(r + 1) * cols, :] = G[at:at + cols, :].astype(bf16)

    for c in st3:
        c.wait()
    if scatter:
        o3 = pl.multiple_of(o2 + lon * n3, 16)
        v = GF[pl.ds(o3, n3), :]
        for d in range(1, L):
            v = v + R3[d - 1].astype(f32)
        GA[pl.ds(o3, n3), :] = v.astype(bf16)
        cs = []
        for d in range(1, L):
            c = rcopy(GA.at[pl.ds(o3, n3)], GA.at[pl.ds(o3, n3)], a3s.at[d - 1], a3r.at[d - 1], {"lon": lax.rem(lon + d, L)})
            c.start()
            cs.append(c)
        for c in cs:
            c.wait()
    else:
        R3[lon] = GB[pl.ds(o2, n2), :]
        v = R3[0].astype(f32)
        for q in range(1, L):
            v = v + R3[q].astype(f32)
        GA[pl.ds(o2, n2), :] = v.astype(bf16)
    cs = []
    for d in range(1, M):
        c = rcopy(GA.at[pl.ds(o2, n2)], GA.at[pl.ds(o2, n2)], a2s.at[d - 1], a2r.at[d - 1], {"member": lax.rem(mem + d, M)})
        c.start()
        cs.append(c)
    for c in cs:
        c.wait()
    c = rcopy(GA.at[pl.ds(o1, n1)], GA.at[pl.ds(o1, n1)], a1s, a1r, {"lat": other})
    c.start()
    c.wait()
    gc_ref[:, :hc] = GA[0:KC, :].astype(f32) * scale
    gc_ref[:, hc:] = GA[KC:2 * KC, :].astype(f32) * scale
    go_ref[...] = GA[2 * KC:total, :fields].astype(f32) * scale


def local(mesh_shape, latent, target, quadrature, widths, conv_weight, output_weight):
    rows, cols, C = latent.shape[1:]
    K, _, taps_lat, taps_lon = quadrature.shape
    half = taps_lon // 2
    fields = output_weight.shape[1]
    L, M = mesh_shape["lon"], mesh_shape["member"]
    lats = mesh_shape["lat"]
    assert lats == 2
    pitch, slots, window, span = dims_of(rows, cols, taps_lat, half)
    n = rows * cols
    radius = taps_lat // 2
    hh = radius * half
    start = lax.axis_index("lat") * rows
    quad = lax.dynamic_slice_in_dim(quadrature, start, rows, 1)
    wid = lax.dynamic_slice_in_dim(widths, start, rows, 0)
    keep = jnp.abs(jnp.arange(taps_lon) - half)[None, :] <= wid[:, None]
    psi = jnp.where(keep[None, :, None, :], quad, jnp.zeros_like(quad)).astype(f32)
    base = jnp.pad(psi, ((0, 8 - K), (0, 0), (0, 0), (0, pitch - taps_lon))).transpose(1, 0, 2, 3)
    base = base.reshape(rows * 8, taps_lat * pitch)
    lead = 16 - half
    base = jnp.pad(base, ((0, 0), (lead, window - lead - taps_lat * pitch)))
    scale = 1.0 / math.sqrt(M * rows * lats * cols * L)
    sizes = (rows, cols, C, K, taps_lat, half, L, M, fields, scale)
    total = 2 * K * C + C
    n1 = total // 2
    n2 = n1 // M
    scatter = n2 % (16 * L) == 0
    r3 = (L - 1, n2 // L, 128) if scatter else (L, n2, 128)
    V = pltpu.VMEM
    D = pltpu.SemaphoreType.DMA
    scratch = [
        V((rows, K * cols, window), bf16), V((span, C), bf16), V((span, C), f32),
        V((n, K * C), bf16), V((n, K * C), bf16), V((n, C), f32), V((n, C), bf16),
        V((n, 128), bf16), V((M - 1, n, 128), bf16), V((C, 128), bf16), V((n, 128), bf16), V((n, C), bf16),
        V((total, 128), f32), V((total, 128), bf16), V((total, 128), bf16),
        V((rows * half, C), bf16), V((rows * half, C), bf16),
        V((slots * half, C), bf16), V((slots * half, C), bf16), V((radius * cols, C), bf16),
        V((slots * half, C), bf16), V((slots * half, C), bf16), V((radius * cols, C), bf16),
        V((rows * half, C), bf16), V((rows * half, C), bf16), V((radius * cols, C), bf16),
        V((hh, C), bf16), V((hh, C), bf16),
        V((n1, 128), bf16), V((M - 1, n2, 128), bf16), V(r3, bf16),
        D((5,)), D((5,)), D((M - 1, CHUNKS)), D((M - 1, CHUNKS)), D((5,)), D((5,)),
        D(()), D(()), D((M - 1,)), D((M - 1,)), D((L - 1,)), D((L - 1,)),
        D((L - 1,)), D((L - 1,)), D((M - 1,)), D((M - 1,)), D(()), D(()),
    ]
    spec = pl.BlockSpec(memory_space=pltpu.VMEM)
    gl, gc, go = pl.pallas_call(
        functools.partial(kernel, sizes),
        out_shape=(jax.ShapeDtypeStruct((n, C), bf16), jax.ShapeDtypeStruct((K * C, C), f32),
                   jax.ShapeDtypeStruct((C, fields), f32)),
        in_specs=[spec] * 5,
        out_specs=(spec,) * 3,
        scratch_shapes=scratch,
        compiler_params=pltpu.CompilerParams(
            collective_id=0, has_side_effects=True, vmem_limit_bytes=48 * 1024 * 1024),
    )(latent.reshape(n, C), target.reshape(n, fields), base, conv_weight, output_weight)
    return gl.reshape(1, rows, cols, C), gc, go


def solution(mesh):
    in_specs = (
        P(("groups", "member"), "lat", "lon", None),
        P(("groups", "lat"), "lon", None),
        P(),
        P(),
        P(),
        P(),
    )
    out_specs = (P(("groups", "member"), "lat", "lon", None), P("groups", None), P("groups", None))
    body = functools.partial(local, dict(mesh.shape))
    return jax.shard_map(body, mesh=mesh, in_specs=in_specs, out_specs=out_specs, check_vma=False)
```

time: 200 us -> 50.6 us (0.25)
  waiting for transfers between devices: 90.3 us -> 0 us
  Pallas kernels: 0 us -> 43.2 us
  matrix products: 42 us -> 0 us
  starting transfers between devices: 14.6 us -> 0 us
  between operations: 14.2 us -> 0.74 us
  other arithmetic: 10.3 us -> 0.3 us
  blocking collectives: 9.04 us -> 0 us
  local copies, waits for them, and re-layouts: 14.9 us -> 6.11 us
  loops' own time: 3.04 us -> 0 us
    psum x1 -> x0, waiting for transfers between devices: 75.7 us -> none  [local(): lax.psum((conv_local, out_local), ('lon', 'lat', 'member'))]
    pallas_call x0 -> x1, Pallas kernels: none -> 43.2 us  [local(): pl.pallas_call(functools.partial(kernel, sizes), out_shape=(jax.ShapeDtyp...]
    dot_general x30 -> x0, matrix products: 42 us -> none  [the longest x10 19.2 us: adjoint_block(): jnp.einsum('iksq,iskc->iqc', toeplitz, window, preferred_element_type=jnp...]
    ppermute x8 -> x0, waiting for transfers between devices: 14.5 us -> none  [the longest x4 8.61 us: extended(): lax.ppermute(lax.slice_in_dim(block, block.shape[dim] - width, None, axis...]
    ppermute x8 -> x0, starting transfers between devices: 14.5 us -> none  [the longest x4 7.92 us: extended(): lax.ppermute(lax.slice_in_dim(block, 0, width, axis=dim), axis, backward)]
    all_gather x1 -> x0, blocking collectives: 9.04 us -> none  [local(): lax.all_gather(predicted_state, 'member', axis=0, tiled=True)]
    mul x3 -> x0, other arithmetic: 3.8 us -> none  [the longest x1 2.26 us: local(): grad_conv = conv_total * norm_scale]
    dynamic_update_slice x2 -> x0, local copies, waits for them, and re-layouts: 3.6 us -> none  [local(): lax.map(basis_block, jnp.arange(block_count))]
  transfers between devices with their start and end apart: 9 -> 0, of which waited for: 4 -> 0; matrix products, arithmetic and copies ran while one was open for 4% -> 0% of each run, Pallas kernels for 0% -> 0%
where the time goes in v1:
time: 50.6 us; the launch traced here: 50.4 us
  Pallas kernels  43.2 us (85%)
  local copies, waits for them, and re-layouts  6.11 us (12%)
  between operations  0.74 us (1%)
    pallas_call x1, Pallas kernels, local(): pl.pallas_call(functools.partial(kernel, sizes), out_shape=(jax.ShapeDtyp...  43.2 us
    unnamed x12, local copies, waits for them, and re-layouts  4.18 us

profile of v1, /device:TPU:0, one launch (start us, length us, event | category | flops | bytes accessed | tf_op | source)
XLA Modules:
  0.0 50.4 jit_solution(1153091077262090413)
XLA Ops:
  0.6 0.0 copy-start.3
  0.6 0.8 %dynamic_slice.6 = s32[16]{0:T(128)S(1)} dynamic-slice(s32[32]{0:T(128)} %param.9, s32[]{:T(128)S(6)} %select_n.8), dynamic_slice_sizes={16} | dynamic-slice | bytes 132 | tf_op jit(solution)/shard_map/dynamic_slice | solution.py:312
  1.4 0.1 broadcast_compare_fusion
  1.5 0.9 %copy.13.ow_ref = bf16[256,72]{1,0:T(8,128)(2,1)S(1)} copy(bf16[256,72]{0,1:T(8,128)(2,1)} %param.11) | data formatting | bytes 73728 | tf_op args[5]
  2.4 0.0 copy-done.3
  2.4 0.1 dynamic-slice_select_fusion
  2.5 0.1 pad_bitcast_fusion
  2.6 0.0 copy-start.1
  2.7 0.0 copy-start.2
  2.7 0.9 %copy.12 = bf16[16,8,5,80]{3,2,1,0:T(8,128)(2,1)S(1)} copy(bf16[16,8,5,80]{0,1,3,2:T(8,128)(2,1)S(1)} %pad_bitcast_fusion) | data formatting | bytes 204800 | tf_op jit(solution)/shard_map/transpose | solution.py:315
  3.6 0.0 copy-start
  3.6 0.2 reshape.52
  3.7 0.1 pad_convert_fusion.base_ref
  3.8 0.0 copy-done.1
  3.9 0.0 copy-done.2
  3.9 0.8 %copy-done = bf16[1,16,64,256]{3,2,1,0:T(8,128)(2,1)S(1)} copy-done((bf16[1,16,64,256]{3,2,1,0:T(8,128)(2,1)S(1)}, bf16[1,16,64,256]{3,2,1,0:T(8,128)(2,1)}, u32[]{:S(2)}) %copy-start) | copy-done | bytes 524312
  4.7 43.2 %shard_map.85 = (bf16[1024,256]{1,0:T(8,128)(2,1)S(1)}, f32[1024,256]{1,0:T(8,128)S(1)}, f32[256,72]{1,0:T(8,128)S(1)}) custom-call(bf16[1024,256]{1,0:T(8,128)(2,1)S(1)} %bitcast.6, f32[1024,72]{1,0:T(8,128)S(1)} %bitcast.7, f32[128,512]{1,0:T(8,128)S(1)} %pad_convert_fusion.base_ref, bf16[1024,256]{1,0:T(8,128)(2,1)S(1)} %copy-done.2, ...), custom_call_target="tpu_custom_call" | custom-call | tf_op jit(solution)/shard_map/pallas_call | solution.py:344
  47.9 0.7 %copy.14 = f32[256,72]{0,1:T(8,128)} copy(f32[256,72]{1,0:T(8,128)S(1)} %get-tuple-element.14) | data formatting | bytes 147456
  48.6 0.8 %copy.17 = bf16[1,16,64,256]{3,2,1,0:T(8,128)(2,1)} copy(bf16[1,16,64,256]{3,2,1,0:T(8,128)(2,1)S(1)} %bitcast.5) | data formatting | bytes 1048576
  49.4 1.0 %copy.18 = f32[1024,256]{1,0:T(8,128)} copy(f32[1024,256]{1,0:T(8,128)S(1)} %get-tuple-element.19) | data formatting | bytes 2097152
  (1 shorter events, 0.0 us)
Async XLA Ops:
  0.6 1.7 %copy-start.3 = (bf16[4,32,5,17]{1,0,3,2:T(4,128)(2,1)S(1)}, bf16[4,32,5,17]{1,0,3,2:T(4,128)(2,1)}, u32[]{:S(2)}) copy-start(bf16[4,32,5,17]{1,0,3,2:T(4,128)(2,1)} %param.8) | copy-start | bytes 65284
  2.6 1.2 %copy-start.1 = (f32[16,64,72]{2,1,0:T(8,128)S(1)}, f32[16,64,72]{2,1,0:T(8,128)}, u32[]{:S(2)}) copy-start(f32[16,64,72]{2,1,0:T(8,128)} %param.7) | copy-start | bytes 884740
  2.7 1.2 %copy-start.2 = (bf16[1024,256]{1,0:T(8,128)(2,1)S(1)}, bf16[1024,256]{1,0:T(8,128)(2,1)}, u32[]{:S(2)}) copy-start(bf16[1024,256]{1,0:T(8,128)(2,1)} %cw_ref.1) | copy-start | bytes 1572868
  3.6 1.1 %copy-start = (bf16[1,16,64,256]{3,2,1,0:T(8,128)(2,1)S(1)}, bf16[1,16,64,256]{3,2,1,0:T(8,128)(2,1)}, u32[]{:S(2)}) copy-start(bf16[1,16,64,256]{3,2,1,0:T(8,128)(2,1)} %param.6) | copy-start | bytes 1572868

commit v2 on v1

--- a/solution.py
+++ b/solution.py
@@ -13,6 +13,7 @@
 f32 = jnp.float32
 bf16 = jnp.bfloat16
 CHUNKS = 4
+PIECES = 3
 
 
 def slope(d):
@@ -26,8 +27,8 @@
     return pitch, slots, window, (rows - 1) * pitch + window
 
 
-def kernel(sizes, lat_ref, tgt_ref, base_ref, cw_ref, ow_ref, gl_ref, gc_ref, go_ref,
-           T, X, G, basis, BG, DG, mixed, F, FR, wo, pg, hg, GF, GB, GA,
+def kernel(sizes, wid_ref, lat_ref, tgt_ref, q_ref, cw_ref, ow_ref, gl_ref, gc_ref, go_ref,
+           base, FP, T, X, G, basis, BG, DG, mixed, F, FR, wo, pg, hg, GF, GB, GA,
            SL, SR, RL, RR, RC, SL2, SR2, SC2, QL, QR, QC, QLd, QRd, R1, R2, R3,
            hs, hr, fs, fr, as_, ar, s1s, s1r, s2s, s2r, s3s, s3r, a3s, a3r, a2s, a2r, a1s, a1r):
     rows, cols, C, K, taps_lat, half, L, M, fields, scale = sizes
@@ -78,17 +79,29 @@
     for c in halo:
         c.start()
 
+    taps = q_ref.shape[0]
+    taps_lon = taps // taps_lat
+    nlat = 2 * rows
+    tap = lax.broadcasted_iota(jnp.int32, (taps, window), 0)
+    lane = lax.broadcasted_iota(jnp.int32, (taps, window), 1) - (16 - half)
+    tap_a = tap // taps_lon
+    place = (lane == tap_a * pitch + (tap - tap_a * taps_lon)).astype(bf16)
+    base[...] = lax.dot_general(q_ref[...], place, (((0,), (0,)), ((), ())), preferred_element_type=f32)
+    lane1 = lax.broadcasted_iota(jnp.int32, (1, window), 1) - (16 - half)
+    offset = jnp.abs(lane1 - lane1 // pitch * pitch - half)
+
     def build(i, carry):
-        rowsb = base_ref[pl.ds(pl.multiple_of(i * 8, 8), 8), :]
+        row = lat * rows + i
+        keep = offset <= wid_ref[row]
         for k in range(K):
-            line = jnp.broadcast_to(rowsb[k:k + 1, :], (cols, window))
+            line = jnp.where(keep, base[pl.ds(k * nlat + row, 1), :], 0.0)
+            line = jnp.broadcast_to(line, (cols, window))
             T[i, k * cols:(k + 1) * cols, :] = pltpu.roll(line, 0, 1, stride=1, stride_axis=0).astype(bf16)
         return carry
     lax.fori_loop(0, rows, build, 0)
 
     G[...] = jnp.zeros(G.shape, f32)
-    wo[...] = jnp.zeros(wo.shape, bf16)
-    wo[:, :fields] = ow_ref[...]
+    wo[...] = jnp.concatenate([ow_ref[...].astype(f32), jnp.zeros((128 - fields, C), f32)], axis=0).astype(bf16)
     pg[...] = jnp.zeros(pg.shape, bf16)
     X[pl.ds(16 + slots * pitch, span - 16 - slots * pitch), :] = jnp.zeros((span - 16 - slots * pitch, C), bf16)
     for r in range(rows):
@@ -110,6 +123,10 @@
             [rr[r * half:(r + 1) * half], nxt], axis=0).astype(bf16)
 
     c0 = math.sqrt(2 / math.pi)
+    groups = cn // 16
+    lw = fields - 64
+    assert groups * lw == 128
+    pn = cn // 2 + 16
     fcopies = []
     for ch in range(CHUNKS):
         def conv(ii, carry, ch=ch):
@@ -125,10 +142,15 @@
         DG[sl, :] = 0.5 * (1 + t) + 0.5 * h * (1 - t * t) * (c0 * (1 + 3 * 0.044715 * h * h))
         mx = (lat_ref[sl, :].astype(f32) + 0.5 * h * (1 + t)).astype(bf16)
         mixed[sl, :] = mx
-        F[sl, :] = jnp.dot(mx, wo[...], preferred_element_type=f32).astype(bf16)
+        fc = lax.dot_general(mx, wo[...], (((1,), (1,)), ((), ())), preferred_element_type=f32)
+        F[sl, :] = fc.astype(bf16)
+        psl = pl.ds(ch * pn, pn)
+        both = jnp.concatenate([fc[:cn // 2, :64], fc[cn // 2:, :64]], axis=1)
+        rest = jnp.concatenate([fc[g * 16:(g + 1) * 16, 64:fields] for g in range(groups)], axis=1)
+        FP[ch * pn:(ch + 1) * pn, :] = jnp.concatenate([both, rest], axis=0).astype(bf16)
         cs = []
         for d in range(1, M):
-            c = rcopy(F.at[pl.ds(ch * cn, cn)], FR.at[d - 1, pl.ds(ch * cn, cn)], fs.at[d - 1, ch], fr.at[d - 1, ch],
+            c = rcopy(FP.at[psl], FR.at[d - 1, psl], fs.at[d - 1, ch], fr.at[d - 1, ch],
                       {"member": lax.rem(mem + d, M)})
             c.start()
             cs.append(c)
@@ -142,9 +164,15 @@
             c.wait()
         pair = jnp.zeros_like(mine)
         for d in range(1, M):
-            pair = pair + slope(mine - FR[d - 1, sl, :fields].astype(f32))
+            got = FR[d - 1, ch * pn:(ch + 1) * pn, :].astype(f32)
+            body = got[:cn // 2]
+            rest = got[cn // 2:]
+            theirs = jnp.concatenate([
+                jnp.concatenate([body[:, :64], body[:, 64:]], axis=0),
+                jnp.concatenate([rest[:, g * lw:(g + 1) * lw] for g in range(groups)], axis=0)], axis=1)
+            pair = pair + slope(mine - theirs)
         pg[sl, :fields] = (first - pair * (1.0 / (M - 1))).astype(bf16)
-        up = lax.dot_general(pg[sl, :], wo[...], (((1,), (1,)), ((), ())), preferred_element_type=f32)
+        up = jnp.dot(pg[sl, :], wo[...], preferred_element_type=f32)
         for ii in range(per):
             r = ch * per + ii + radius
             G[16 + pitch * r:16 + pitch * r + cols, :] = up[ii * cols:(ii + 1) * cols]
@@ -152,28 +180,41 @@
 
     KC = K * C
     hc = C // 2
-    total = 2 * KC + C
+    total = 2 * KC + 256
+    tc = total // PIECES
+    n1 = tc // 2
+    n2 = n1 // M
+    scatter = n2 % (16 * L) == 0
+    n3 = n2 // L if scatter else n2
+    o1 = [pl.multiple_of(c * tc + lat * n1, 16) for c in range(PIECES)]
+    o1o = [pl.multiple_of(c * tc + other * n1, 16) for c in range(PIECES)]
+    o2 = [pl.multiple_of(o1[c] + mem * n2, 16) for c in range(PIECES)]
     tn = (((0,), (0,)), ((), ()))
+    st1 = []
+
+    def ready(done):
+        while len(st1) < PIECES and (len(st1) + 1) * tc <= done:
+            c = len(st1)
+            copy = rcopy(GB.at[pl.ds(o1o[c], n1)], R1.at[c], s1s.at[c], s1r.at[c], {"lat": other})
+            copy.start()
+            st1.append(copy)
+
     hgv = hg[...]
     for k in range(K):
         g = lax.dot_general(basis[:, k * C:(k + 1) * C], hgv, tn, preferred_element_type=f32)
         for half_id in range(2):
             part = g[:, half_id * hc:(half_id + 1) * hc]
-            at = half_id * KC + k * C
+            at = (2 * k + half_id) * C
             GF[at:at + C, :] = part
             GB[at:at + C, :] = part.astype(bf16)
-    g = lax.dot_general(mixed[...], pg[...], tn, preferred_element_type=f32)
-    GF[2 * KC:total, :] = g
-    GB[2 * KC:total, :] = g.astype(bf16)
-
-    n1 = total // 2
-    n2 = n1 // M
-    scatter = n2 % (16 * L) == 0
-    n3 = n2 // L if scatter else n2
-    o1 = pl.multiple_of(lat * n1, 16)
-    o1o = pl.multiple_of(other * n1, 16)
-    st1 = rcopy(GB.at[pl.ds(o1o, n1)], R1, s1s, s1r, {"lat": other})
-    st1.start()
+        ready(2 * (k + 1) * C)
+    g = lax.dot_general(pg[...], mixed[...], tn, preferred_element_type=f32)
+    for half_id in range(2):
+        part = g[:, half_id * hc:(half_id + 1) * hc]
+        at = 2 * KC + half_id * 128
+        GF[at:at + 128, :] = part
+        GB[at:at + 128, :] = part.astype(bf16)
+    ready(total)
 
     def adjoint(first_row, last_row):
         lo, size = first_row * cols, (last_row - first_row) * cols
@@ -189,22 +230,45 @@
             return carry
         lax.fori_loop(first_row, last_row, body, 0)
 
-    adjoint(0, rows // 2)
-
-    st1.wait()
-    v = GF[pl.ds(o1, n1), :] + R1[...].astype(f32)
-    GF[pl.ds(o1, n1), :] = v
-    GB[pl.ds(o1, n1), :] = v.astype(bf16)
+    quarter = rows // 4
+    adjoint(0, quarter)
     st2 = []
-    for d in range(1, M):
-        q = lax.rem(mem + d, M)
-        c = rcopy(GB.at[pl.ds(pl.multiple_of(o1 + q * n2, 16), n2)], R2.at[d - 1], s2s.at[d - 1], s2r.at[d - 1], {"member": q})
-        c.start()
-        st2.append(c)
-
-    adjoint(rows // 2, rows)
-    for r in range(slots):
-        pass
+    for c in range(PIECES):
+        st1[c].wait()
+        w = pl.ds(o1[c], n1)
+        v = GF[w, :] + R1[c].astype(f32)
+        GF[w, :] = v
+        GB[w, :] = v.astype(bf16)
+        cs = []
+        for d in range(1, M):
+            q = lax.rem(mem + d, M)
+            copy = rcopy(GB.at[pl.ds(pl.multiple_of(o1[c] + q * n2, 16), n2)], R2.at[c, d - 1],
+                         s2s.at[c, d - 1], s2r.at[c, d - 1], {"member": q})
+            copy.start()
+            cs.append(copy)
+        st2.append(cs)
+
+    st3 = []
+    for c in range(PIECES):
+        adjoint((c + 1) * quarter, (c + 2) * quarter)
+        for copy in st2[c]:
+            copy.wait()
+        w = pl.ds(o2[c], n2)
+        v = GF[w, :]
+        for d in range(1, M):
+            v = v + R2[c, d - 1].astype(f32)
+        GF[w, :] = v
+        GB[w, :] = v.astype(bf16)
+        cs = []
+        for d in range(1, L):
+            q = lax.rem(lon + d, L)
+            src = GB.at[pl.ds(pl.multiple_of(o2[c] + q * n3, 16), n3)] if scatter else GB.at[w]
+            dst = R3.at[c, d - 1] if scatter else R3.at[c, lon]
+            copy = rcopy(src, dst, s3s.at[c, d - 1], s3r.at[c, d - 1], {"lon": q})
+            copy.start()
+            cs.append(copy)
+        st3.append(cs)
+
     SR2[...] = jnp.concatenate([G[16 + pitch * r + cols:16 + pitch * r + cols + half, :] for r in range(slots)], axis=0).astype(bf16)
     SL2[...] = jnp.concatenate([G[16 + pitch * r - half:16 + pitch * r, :] for r in range(slots)], axis=0).astype(bf16)
     for r in range(radius):
@@ -220,22 +284,29 @@
     for c in back:
         c.start()
 
-    for c in st2:
-        c.wait()
-    o2 = pl.multiple_of(o1 + mem * n2, 16)
-    v = GF[pl.ds(o2, n2), :]
-    for d in range(1, M):
-        v = v + R2[d - 1].astype(f32)
-    GF[pl.ds(o2, n2), :] = v
-    GB[pl.ds(o2, n2), :] = v.astype(bf16)
-    st3 = []
-    for d in range(1, L):
-        q = lax.rem(lon + d, L)
-        src = GB.at[pl.ds(pl.multiple_of(o2 + q * n3, 16), n3)] if scatter else GB.at[pl.ds(o2, n2)]
-        dst = R3.at[d - 1] if scatter else R3.at[lon]
-        c = rcopy(src, dst, s3s.at[d - 1], s3r.at[d - 1], {"lon": q})
-        c.start()
-        st3.append(c)
+    ag3 = []
+    for c in range(PIECES):
+        for copy in st3[c]:
+            copy.wait()
+        cs = []
+        if scatter:
+            w = pl.ds(pl.multiple_of(o2[c] + lon * n3, 16), n3)
+            v = GF[w, :]
+            for d in range(1, L):
+                v = v + R3[c, d - 1].astype(f32)
+            GA[w, :] = v.astype(bf16)
+            for d in range(1, L):
+                copy = rcopy(GA.at[w], GA.at[w], a3s.at[c, d - 1], a3r.at[c, d - 1], {"lon": lax.rem(lon + d, L)})
+                copy.start()
+                cs.append(copy)
+        else:
+            w = pl.ds(o2[c], n2)
+            R3[c, lon] = GB[w, :]
+            v = R3[c, 0].astype(f32)
+            for q in range(1, L):
+                v = v + R3[c, q].astype(f32)
+            GA[w, :] = v.astype(bf16)
+        ag3.append(cs)
 
     for c in back:
         c.wait()
@@ -255,44 +326,39 @@
         G[w, :] = G[w, :] + qld[r * half:(r + 1) * half]
         w = pl.ds(pl.multiple_of(at + cols - half, 8), half)
         G[w, :] = G[w, :] + qrd[r * half:(r + 1) * half]
+    ag2 = []
+    for c in range(PIECES):
+        for copy in ag3[c]:
+            copy.wait()
+        w = pl.ds(o2[c], n2)
+        cs = []
+        for d in range(1, M):
+            copy = rcopy(GA.at[w], GA.at[w], a2s.at[c, d - 1], a2r.at[c, d - 1], {"member": lax.rem(mem + d, M)})
+            copy.start()
+            cs.append(copy)
+        ag2.append(cs)
     for r in range(rows):
         at = 16 + pitch * (r + radius)
         gl_ref[r * cols:(r + 1) * cols, :] = G[at:at + cols, :].astype(bf16)
 
-    for c in st3:
-        c.wait()
-    if scatter:
-        o3 = pl.multiple_of(o2 + lon * n3, 16)
-        v = GF[pl.ds(o3, n3), :]
-        for d in range(1, L):
-            v = v + R3[d - 1].astype(f32)
-        GA[pl.ds(o3, n3), :] = v.astype(bf16)
-        cs = []
-        for d in range(1, L):
-            c = rcopy(GA.at[pl.ds(o3, n3)], GA.at[pl.ds(o3, n3)], a3s.at[d - 1], a3r.at[d - 1], {"lon": lax.rem(lon + d, L)})
-            c.start()
-            cs.append(c)
-        for c in cs:
-            c.wait()
-    else:
-        R3[lon] = GB[pl.ds(o2, n2), :]
-        v = R3[0].astype(f32)
-        for q in range(1, L):
-            v = v + R3[q].astype(f32)
-        GA[pl.ds(o2, n2), :] = v.astype(bf16)
-    cs = []
-    for d in range(1, M):
-        c = rcopy(GA.at[pl.ds(o2, n2)], GA.at[pl.ds(o2, n2)], a2s.at[d - 1], a2r.at[d - 1], {"member": lax.rem(mem + d, M)})
-        c.start()
-        cs.append(c)
-    for c in cs:
-        c.wait()
-    c = rcopy(GA.at[pl.ds(o1, n1)], GA.at[pl.ds(o1, n1)], a1s, a1r, {"lat": other})
-    c.start()
-    c.wait()
-    gc_ref[:, :hc] = GA[0:KC, :].astype(f32) * scale
-    gc_ref[:, hc:] = GA[KC:2 * KC, :].astype(f32) * scale
-    go_ref[...] = GA[2 * KC:total, :fields].astype(f32) * scale
+    ag1 = []
+    for c in range(PIECES):
+        for copy in ag2[c]:
+            copy.wait()
+        w = pl.ds(o1[c], n1)
+        copy = rcopy(GA.at[w], GA.at[w], a1s.at[c], a1r.at[c], {"lat": other})
+        copy.start()
+        ag1.append(copy)
+    block = 0
+    for c in range(PIECES):
+        ag1[c].wait()
+        while block < 2 * K and (block + 1) * C <= (c + 1) * tc:
+            k, half_id = block // 2, block % 2
+            gc_ref[k * C:(k + 1) * C, half_id * hc:(half_id + 1) * hc] = GA[block * C:(block + 1) * C, :].astype(f32) * scale
+            block += 1
+    for half_id in range(2):
+        at = 2 * KC + half_id * 128
+        go_ref[:, half_id * hc:(half_id + 1) * hc] = GA[at:at + 128, :].astype(f32)[:fields] * scale
 
 
 def local(mesh_shape, latent, target, quadrature, widths, conv_weight, output_weight):
@@ -307,51 +373,45 @@
     n = rows * cols
     radius = taps_lat // 2
     hh = radius * half
-    start = lax.axis_index("lat") * rows
-    quad = lax.dynamic_slice_in_dim(quadrature, start, rows, 1)
-    wid = lax.dynamic_slice_in_dim(widths, start, rows, 0)
-    keep = jnp.abs(jnp.arange(taps_lon) - half)[None, :] <= wid[:, None]
-    psi = jnp.where(keep[None, :, None, :], quad, jnp.zeros_like(quad)).astype(f32)
-    base = jnp.pad(psi, ((0, 8 - K), (0, 0), (0, 0), (0, pitch - taps_lon))).transpose(1, 0, 2, 3)
-    base = base.reshape(rows * 8, taps_lat * pitch)
-    lead = 16 - half
-    base = jnp.pad(base, ((0, 0), (lead, window - lead - taps_lat * pitch)))
+    q2 = quadrature.transpose(2, 3, 0, 1).reshape(taps_lat * taps_lon, K * rows * lats)
     scale = 1.0 / math.sqrt(M * rows * lats * cols * L)
     sizes = (rows, cols, C, K, taps_lat, half, L, M, fields, scale)
-    total = 2 * K * C + C
-    n1 = total // 2
+    total = 2 * K * C + 256
+    n1 = total // PIECES // 2
     n2 = n1 // M
     scatter = n2 % (16 * L) == 0
-    r3 = (L - 1, n2 // L, 128) if scatter else (L, n2, 128)
+    r3 = (PIECES, L - 1, n2 // L, 128) if scatter else (PIECES, L, n2, 128)
+    pn = n // CHUNKS // 2 + 16
     V = pltpu.VMEM
     D = pltpu.SemaphoreType.DMA
     scratch = [
+        V((K * rows * lats, window), f32), V((CHUNKS * pn, 128), bf16),
         V((rows, K * cols, window), bf16), V((span, C), bf16), V((span, C), f32),
         V((n, K * C), bf16), V((n, K * C), bf16), V((n, C), f32), V((n, C), bf16),
-        V((n, 128), bf16), V((M - 1, n, 128), bf16), V((C, 128), bf16), V((n, 128), bf16), V((n, C), bf16),
+        V((n, 128), bf16), V((M - 1, CHUNKS * pn, 128), bf16), V((128, C), bf16), V((n, 128), bf16), V((n, C), bf16),
         V((total, 128), f32), V((total, 128), bf16), V((total, 128), bf16),
         V((rows * half, C), bf16), V((rows * half, C), bf16),
         V((slots * half, C), bf16), V((slots * half, C), bf16), V((radius * cols, C), bf16),
         V((slots * half, C), bf16), V((slots * half, C), bf16), V((radius * cols, C), bf16),
         V((rows * half, C), bf16), V((rows * half, C), bf16), V((radius * cols, C), bf16),
         V((hh, C), bf16), V((hh, C), bf16),
-        V((n1, 128), bf16), V((M - 1, n2, 128), bf16), V(r3, bf16),
+        V((PIECES, n1, 128), bf16), V((PIECES, M - 1, n2, 128), bf16), V(r3, bf16),
         D((5,)), D((5,)), D((M - 1, CHUNKS)), D((M - 1, CHUNKS)), D((5,)), D((5,)),
-        D(()), D(()), D((M - 1,)), D((M - 1,)), D((L - 1,)), D((L - 1,)),
-        D((L - 1,)), D((L - 1,)), D((M - 1,)), D((M - 1,)), D(()), D(()),
+        D((PIECES,)), D((PIECES,)), D((PIECES, M - 1)), D((PIECES, M - 1)), D((PIECES, L - 1)), D((PIECES, L - 1)),
+        D((PIECES, L - 1)), D((PIECES, L - 1)), D((PIECES, M - 1)), D((PIECES, M - 1)), D((PIECES,)), D((PIECES,)),
     ]
     spec = pl.BlockSpec(memory_space=pltpu.VMEM)
     gl, gc, go = pl.pallas_call(
         functools.partial(kernel, sizes),
         out_shape=(jax.ShapeDtypeStruct((n, C), bf16), jax.ShapeDtypeStruct((K * C, C), f32),
-                   jax.ShapeDtypeStruct((C, fields), f32)),
-        in_specs=[spec] * 5,
+                   jax.ShapeDtypeStruct((fields, C), f32)),
+        in_specs=[pl.BlockSpec(memory_space=pltpu.SMEM)] + [spec] * 5,
         out_specs=(spec,) * 3,
         scratch_shapes=scratch,
         compiler_params=pltpu.CompilerParams(
             collective_id=0, has_side_effects=True, vmem_limit_bytes=48 * 1024 * 1024),
-    )(latent.reshape(n, C), target.reshape(n, fields), base, conv_weight, output_weight)
-    return gl.reshape(1, rows, cols, C), gc, go
+    )(widths, latent.reshape(n, C), target.reshape(n, fields), q2, conv_weight, output_weight.T)
+    return gl.reshape(1, rows, cols, C), gc, go.T
 
 
 def solution(mesh):

time: 50.6 us -> 49 us (0.968)
  Pallas kernels: 43.2 us -> 41.5 us
    pallas_call x1, Pallas kernels: 43.2 us -> 41.5 us  [local(): pl.pallas_call(functools.partial(kernel, sizes), out_shape=(jax.ShapeDtyp...]
    unnamed x12 -> x13, local copies, waits for them, and re-layouts: 4.18 us -> 5.52 us
    transpose x2 -> x0, local copies, waits for them, and re-layouts: 1 us -> none  [local(): jnp.pad(psi, ((0, 8 - K), (0, 0), (0, 0), (0, pitch - taps_lon)))]
    reshape x1, local copies, waits for them, and re-layouts: 0.16 us -> 1.03 us  [local(): quadrature.transpose(2, 3, 0, 1)]
    dynamic_slice x1 -> x0, local copies, waits for them, and re-layouts: 0.76 us -> none  [local(): wid = lax.dynamic_slice_in_dim(widths, start, rows, 0)]
where the time goes in v2:
time: 49 us; the launch traced here: 48.7 us
  Pallas kernels  41.5 us (85%)
  local copies, waits for them, and re-layouts  6.55 us (13%)
  between operations  0.68 us (1%)
    pallas_call x1, Pallas kernels, local(): pl.pallas_call(functools.partial(kernel, sizes), out_shape=(jax.ShapeDtyp...  41.5 us
    unnamed x13, local copies, waits for them, and re-layouts  5.52 us
    reshape x1, local copies, waits for them, and re-layouts, local(): quadrature.transpose(2, 3, 0, 1)  1.03 us

profile of v2, /device:TPU:0, one launch (start us, length us, event | category | flops | bytes accessed | tf_op | source)
XLA Modules:
  0.0 48.7 jit_solution(5855686704218894648)
XLA Ops:
  0.6 0.0 copy-start.3
  0.6 0.0 copy-start.4
  0.7 1.0 %reshape.20.q_ref = bf16[85,128]{1,0:T(8,128)(2,1)S(1)} reshape(bf16[5,17,4,32]{3,2,1,0:T(4,128)(2,1)} %bitcast.11) | data formatting | bytes 43520 | tf_op jit(solution)/shard_map/reshape | solution.py:376
  1.7 0.0 copy-done.3
  1.7 0.0 copy-done.4
  1.7 0.0 copy-start
  1.7 1.0 %copy-done = bf16[1,16,64,256]{3,2,1,0:T(8,128)(2,1)S(1)} copy-done((bf16[1,16,64,256]{3,2,1,0:T(8,128)(2,1)S(1)}, bf16[1,16,64,256]{3,2,1,0:T(8,128)(2,1)}, u32[]{:S(2)}) %copy-start) | copy-done | bytes 524312
  2.7 0.0 copy-start.1
  2.7 1.0 %copy-done.1 = f32[16,64,72]{2,1,0:T(8,128)S(1)} copy-done((f32[16,64,72]{2,1,0:T(8,128)S(1)}, f32[16,64,72]{2,1,0:T(8,128)}, u32[]{:S(2)}) %copy-start.1) | copy-done | bytes 294936
  3.8 0.0 copy-start.2
  3.8 1.0 %copy-done.2 = bf16[1024,256]{1,0:T(8,128)(2,1)S(1)} copy-done((bf16[1024,256]{1,0:T(8,128)(2,1)S(1)}, bf16[1024,256]{1,0:T(8,128)(2,1)}, u32[]{:S(2)}) %copy-start.2) | copy-done | bytes 524312
  4.8 41.5 %shard_map.85 = (bf16[1024,256]{1,0:T(8,128)(2,1)S(1)}, f32[1024,256]{1,0:T(8,128)S(1)}, f32[72,256]{1,0:T(8,128)S(1)}) custom-call(s32[32]{0:T(128)S(1)} %copy-done.4, bf16[1024,256]{1,0:T(8,128)(2,1)S(1)} %bitcast.6, f32[1024,72]{1,0:T(8,128)S(1)} %bitcast.7, bf16[85,128]{1,0:T(8,128)(2,1)S(1)} %reshape.20.q_ref, bf16[1024,256]{1,0:T(8,128)(2,1)S(1)} %copy-done.2, ...), custom_call_target="tpu_custom_call" | custom-call | tf_op jit(solution)/shard_map/pallas_call | solution.py:404
  46.3 0.8 %copy.12 = bf16[1,16,64,256]{3,2,1,0:T(8,128)(2,1)} copy(bf16[1,16,64,256]{3,2,1,0:T(8,128)(2,1)S(1)} %bitcast.8) | data formatting | bytes 1048576
  47.1 1.0 %copy.13 = f32[1024,256]{1,0:T(8,128)} copy(f32[1024,256]{1,0:T(8,128)S(1)} %get-tuple-element.13) | data formatting | bytes 2097152
  48.1 0.6 %copy.14 = f32[256,72]{0,1:T(8,128)} copy(f32[256,72]{0,1:T(8,128)S(1)} %bitcast.9) | data formatting | bytes 147456
Async XLA Ops:
  0.6 1.1 %copy-start.3 = (bf16[256,72]{0,1:T(8,128)(2,1)S(1)}, bf16[256,72]{0,1:T(8,128)(2,1)}, u32[]{:S(2)}) copy-start(bf16[256,72]{0,1:T(8,128)(2,1)} %param.11) | copy-start | bytes 110596
  0.6 1.1 %copy-start.4 = (s32[32]{0:T(128)S(1)}, s32[32]{0:T(128)}, u32[]{:S(2)}) copy-start(s32[32]{0:T(128)} %wid_ref.1) | copy-start | bytes 388
  1.7 1.0 %copy-start = (bf16[1,16,64,256]{3,2,1,0:T(8,128)(2,1)S(1)}, bf16[1,16,64,256]{3,2,1,0:T(8,128)(2,1)}, u32[]{:S(2)}) copy-start(bf16[1,16,64,256]{3,2,1,0:T(8,128)(2,1)} %param.6) | copy-start | bytes 1572868
  2.7 1.0 %copy-start.1 = (f32[16,64,72]{2,1,0:T(8,128)S(1)}, f32[16,64,72]{2,1,0:T(8,128)}, u32[]{:S(2)}) copy-start(f32[16,64,72]{2,1,0:T(8,128)} %param.7) | copy-start | bytes 884740
  3.8 1.0 %copy-start.2 = (bf16[1024,256]{1,0:T(8,128)(2,1)S(1)}, bf16[1024,256]{1,0:T(8,128)(2,1)}, u32[]{:S(2)}) copy-start(bf16[1024,256]{1,0:T(8,128)(2,1)} %cw_ref.1) | copy-start | bytes 1572868

commit v3 on v2

--- a/solution.py
+++ b/solution.py
@@ -27,8 +27,8 @@
     return pitch, slots, window, (rows - 1) * pitch + window
 
 
-def kernel(sizes, wid_ref, lat_ref, tgt_ref, q_ref, cw_ref, ow_ref, gl_ref, gc_ref, go_ref,
-           base, FP, T, X, G, basis, BG, DG, mixed, F, FR, wo, pg, hg, GF, GB, GA,
+def kernel(sizes, wid_ref, lat_hbm, tgt_hbm, q_ref, cw_hbm, ow_ref, gl_ref, gc_ref, go_ref,
+           lat_ref, tgt_ref, cw_ref, ins, base, FP, T, X, G, basis, BG, DG, mixed, F, FR, wo, pg, hg, GF, GB, GA,
            SL, SR, RL, RR, RC, SL2, SR2, SC2, QL, QR, QC, QLd, QRd, R1, R2, R3,
            hs, hr, fs, fr, as_, ar, s1s, s1r, s2s, s2r, s3s, s3r, a3s, a3r, a2s, a2r, a1s, a1r):
     rows, cols, C, K, taps_lat, half, L, M, fields, scale = sizes
@@ -49,6 +49,10 @@
         return pltpu.make_async_remote_copy(
             src_ref=src, dst_ref=dst, send_sem=ss, recv_sem=rs, device_id=dev, device_id_type=MESH)
 
+    loads = [pltpu.make_async_copy(src, dst, ins.at[i]) for i, (src, dst) in enumerate(
+        [(lat_hbm, lat_ref), (cw_hbm, cw_ref), (tgt_hbm, tgt_ref)])]
+    for c in loads:
+        c.start()
     barrier = pltpu.get_barrier_semaphore()
     peers = [{"lat": other}, {"lat": other, "lon": left}, {"lat": other, "lon": right}]
     peers += [{"lon": lax.rem(lon + d, L)} for d in range(1, L)]
@@ -56,6 +60,7 @@
     for dev in peers:
         pl.semaphore_signal(barrier, inc=1, device_id=dev, device_id_type=MESH)
 
+    loads[0].wait()
     lat3 = lat_ref[...].astype(f32).reshape(rows, cols, C)
     SL[...] = lat3[:, :half].reshape(rows * half, C).astype(bf16)
     SR[...] = lat3[:, cols - half:].reshape(rows * half, C).astype(bf16)
@@ -122,6 +127,8 @@
         X[16 + pitch * r + cols:16 + pitch * (r + 1), :] = jnp.concatenate(
             [rr[r * half:(r + 1) * half], nxt], axis=0).astype(bf16)
 
+    loads[1].wait()
+    loads[2].wait()
     c0 = math.sqrt(2 / math.pi)
     groups = cn // 16
     lw = fields - 64
@@ -385,6 +392,7 @@
     V = pltpu.VMEM
     D = pltpu.SemaphoreType.DMA
     scratch = [
+        V((n, C), bf16), V((n, fields), f32), V((K * C, C), bf16), D((3,)),
         V((K * rows * lats, window), f32), V((CHUNKS * pn, 128), bf16),
         V((rows, K * cols, window), bf16), V((span, C), bf16), V((span, C), f32),
         V((n, K * C), bf16), V((n, K * C), bf16), V((n, C), f32), V((n, C), bf16),
@@ -401,15 +409,16 @@
         D((PIECES, L - 1)), D((PIECES, L - 1)), D((PIECES, M - 1)), D((PIECES, M - 1)), D((PIECES,)), D((PIECES,)),
     ]
     spec = pl.BlockSpec(memory_space=pltpu.VMEM)
+    far = pl.BlockSpec(memory_space=pltpu.HBM)
     gl, gc, go = pl.pallas_call(
         functools.partial(kernel, sizes),
         out_shape=(jax.ShapeDtypeStruct((n, C), bf16), jax.ShapeDtypeStruct((K * C, C), f32),
                    jax.ShapeDtypeStruct((fields, C), f32)),
-        in_specs=[pl.BlockSpec(memory_space=pltpu.SMEM)] + [spec] * 5,
+        in_specs=[pl.BlockSpec(memory_space=pltpu.SMEM), far, far, spec, far, spec],
         out_specs=(spec,) * 3,
         scratch_shapes=scratch,
         compiler_params=pltpu.CompilerParams(
-            collective_id=0, has_side_effects=True, vmem_limit_bytes=48 * 1024 * 1024),
+            collective_id=0, has_side_effects=True, vmem_limit_bytes=63 * 1024 * 1024),
     )(widths, latent.reshape(n, C), target.reshape(n, fields), q2, conv_weight, output_weight.T)
     return gl.reshape(1, rows, cols, C), gc, go.T
 

time: 49 us -> 49.1 us (level)
  Pallas kernels: 41.5 us -> 42.9 us
  local copies, waits for them, and re-layouts: 6.55 us -> 5.21 us
    unnamed x13 -> x7, local copies, waits for them, and re-layouts: 5.52 us -> 3.58 us
    pallas_call x1, Pallas kernels: 41.5 us -> 42.9 us  [local(): pl.pallas_call(functools.partial(kernel, sizes), out_shape=(jax.ShapeDtyp...]
    reshape x1, local copies, waits for them, and re-layouts: 1.03 us -> 1.63 us  [local(): quadrature.transpose(2, 3, 0, 1)]
where the time goes in v3:
time: 49.1 us; the launch traced here: 48.8 us
  Pallas kernels  42.9 us (87%)
  local copies, waits for them, and re-layouts  5.21 us (11%)
  between operations  0.65 us (1%)
    pallas_call x1, Pallas kernels, local(): pl.pallas_call(functools.partial(kernel, sizes), out_shape=(jax.ShapeDtyp...  42.9 us
    unnamed x7, local copies, waits for them, and re-layouts  3.58 us
    reshape x1, local copies, waits for them, and re-layouts, local(): quadrature.transpose(2, 3, 0, 1)  1.63 us

profile of v3, /device:TPU:0, one launch (start us, length us, event | category | flops | bytes accessed | tf_op | source)
XLA Modules:
  0.0 48.8 jit_solution(4083080881076941918)
XLA Ops:
  0.6 1.6 %reshape.20.q_ref = bf16[85,128]{1,0:T(8,128)(2,1)} reshape(bf16[5,17,4,32]{3,2,1,0:T(4,128)(2,1)} %bitcast.9) | data formatting | bytes 43520 | tf_op jit(solution)/shard_map/reshape | solution.py:383
  2.3 42.9 %shard_map.85 = (bf16[1024,256]{1,0:T(8,128)(2,1)}, f32[1024,256]{1,0:T(8,128)}, f32[72,256]{1,0:T(8,128)}) custom-call(s32[32]{0:T(128)} %wid_ref.1, bf16[1024,256]{1,0:T(8,128)(2,1)} %bitcast.6, f32[1024,72]{1,0:T(8,128)} %bitcast.7, bf16[85,128]{1,0:T(8,128)(2,1)} %reshape.20.q_ref, bf16[1024,256]{1,0:T(8,128)(2,1)} %cw_hbm.1, bf16[72,256]{1,0:T(8,128)(2,1)} %bitcast.11), custom_call_target="tpu_custom_call" | custom-call | tf_op jit(solution)/shard_map/pallas_call | solution.py:413
  45.2 0.0 copy-start
  45.2 2.0 %copy.12 = bf16[1,16,64,256]{3,2,1,0:T(8,128)(2,1)} copy(bf16[1,16,64,256]{3,2,1,0:T(8,128)(2,1)} %bitcast.8) | data formatting | bytes 1048576
  47.2 0.0 copy-done
  47.2 0.0 copy-start.1
  47.2 1.0 %copy.13 = f32[1024,256]{1,0:T(8,128)} copy(f32[1024,256]{1,0:T(8,128)S(1)} %copy-done) | data formatting | bytes 2097152
  48.1 0.0 copy-done.1
  48.2 0.6 %copy.14 = f32[256,72]{0,1:T(8,128)} copy(f32[256,72]{0,1:T(8,128)S(1)} %bitcast.10) | data formatting | bytes 147456
Async XLA Ops:
  45.2 2.0 %copy-start = (f32[1024,256]{1,0:T(8,128)S(1)}, f32[1024,256]{1,0:T(8,128)}, u32[]{:S(2)}) copy-start(f32[1024,256]{1,0:T(8,128)} %get-tuple-element.13) | copy-start | bytes 3145732
  47.2 1.0 %copy-start.1 = (f32[72,256]{1,0:T(8,128)S(1)}, f32[72,256]{1,0:T(8,128)}, u32[]{:S(2)}) copy-start(f32[72,256]{1,0:T(8,128)} %get-tuple-element.8) | copy-start | bytes 221188

commit v4 on v3

--- a/solution.py
+++ b/solution.py
@@ -315,6 +315,17 @@
             GA[w, :] = v.astype(bf16)
         ag3.append(cs)
 
+    ag2 = []
+    for c in range(PIECES):
+        for copy in ag3[c]:
+            copy.wait()
+        w = pl.ds(o2[c], n2)
+        cs = []
+        for d in range(1, M):
+            copy = rcopy(GA.at[w], GA.at[w], a2s.at[c, d - 1], a2r.at[c, d - 1], {"member": lax.rem(mem + d, M)})
+            copy.start()
+            cs.append(copy)
+        ag2.append(cs)
     for c in back:
         c.wait()
     ql = QL[...].astype(f32)
@@ -333,17 +344,6 @@
         G[w, :] = G[w, :] + qld[r * half:(r + 1) * half]
         w = pl.ds(pl.multiple_of(at + cols - half, 8), half)
         G[w, :] = G[w, :] + qrd[r * half:(r + 1) * half]
-    ag2 = []
-    for c in range(PIECES):
-        for copy in ag3[c]:
-            copy.wait()
-        w = pl.ds(o2[c], n2)
-        cs = []
-        for d in range(1, M):
-            copy = rcopy(GA.at[w], GA.at[w], a2s.at[c, d - 1], a2r.at[c, d - 1], {"member": lax.rem(mem + d, M)})
-            copy.start()
-            cs.append(copy)
-        ag2.append(cs)
     for r in range(rows):
         at = 16 + pitch * (r + radius)
         gl_ref[r * cols:(r + 1) * cols, :] = G[at:at + cols, :].astype(bf16)

time: 49.1 us -> 48.4 us (0.986)
  Pallas kernels: 42.9 us -> 42.3 us
    pallas_call x1, Pallas kernels: 42.9 us -> 42.3 us  [local(): pl.pallas_call(functools.partial(kernel, sizes), out_shape=(jax.ShapeDtyp...]
where the time goes in v4:
time: 48.4 us; the launch traced here: 48.1 us
  Pallas kernels  42.3 us (87%)
  local copies, waits for them, and re-layouts  5.21 us (11%)
  between operations  0.65 us (1%)
    pallas_call x1, Pallas kernels, local(): pl.pallas_call(functools.partial(kernel, sizes), out_shape=(jax.ShapeDtyp...  42.3 us
    unnamed x7, local copies, waits for them, and re-layouts  3.58 us
    reshape x1, local copies, waits for them, and re-layouts, local(): quadrature.transpose(2, 3, 0, 1)  1.63 us

profile of v4, /device:TPU:0, one launch (start us, length us, event | category | flops | bytes accessed | tf_op | source)
XLA Modules:
  0.0 48.1 jit_solution(13994840222028427026)
XLA Ops:
  0.6 1.6 %reshape.20.q_ref = bf16[85,128]{1,0:T(8,128)(2,1)} reshape(bf16[5,17,4,32]{3,2,1,0:T(4,128)(2,1)} %bitcast.9) | data formatting | bytes 43520 | tf_op jit(solution)/shard_map/reshape | solution.py:383
  2.3 42.3 %shard_map.85 = (bf16[1024,256]{1,0:T(8,128)(2,1)}, f32[1024,256]{1,0:T(8,128)}, f32[72,256]{1,0:T(8,128)}) custom-call(s32[32]{0:T(128)} %wid_ref.1, bf16[1024,256]{1,0:T(8,128)(2,1)} %bitcast.6, f32[1024,72]{1,0:T(8,128)} %bitcast.7, bf16[85,128]{1,0:T(8,128)(2,1)} %reshape.20.q_ref, bf16[1024,256]{1,0:T(8,128)(2,1)} %cw_hbm.1, bf16[72,256]{1,0:T(8,128)(2,1)} %bitcast.11), custom_call_target="tpu_custom_call" | custom-call | tf_op jit(solution)/shard_map/pallas_call | solution.py:413
  44.5 0.0 copy-start
  44.6 2.0 %copy.12 = bf16[1,16,64,256]{3,2,1,0:T(8,128)(2,1)} copy(bf16[1,16,64,256]{3,2,1,0:T(8,128)(2,1)} %bitcast.8) | data formatting | bytes 1048576
  46.5 0.0 copy-done
  46.5 0.0 copy-start.1
  46.5 1.0 %copy.13 = f32[1024,256]{1,0:T(8,128)} copy(f32[1024,256]{1,0:T(8,128)S(1)} %copy-done) | data formatting | bytes 2097152
  47.5 0.0 copy-done.1
  47.5 0.6 %copy.14 = f32[256,72]{0,1:T(8,128)} copy(f32[256,72]{0,1:T(8,128)S(1)} %bitcast.10) | data formatting | bytes 147456
Async XLA Ops:
  44.5 2.0 %copy-start = (f32[1024,256]{1,0:T(8,128)S(1)}, f32[1024,256]{1,0:T(8,128)}, u32[]{:S(2)}) copy-start(f32[1024,256]{1,0:T(8,128)} %get-tuple-element.13) | copy-start | bytes 3145732
  46.5 1.0 %copy-start.1 = (f32[72,256]{1,0:T(8,128)S(1)}, f32[72,256]{1,0:T(8,128)}, u32[]{:S(2)}) copy-start(f32[72,256]{1,0:T(8,128)} %get-tuple-element.8) | copy-start | bytes 221188
